TPU v7x, 512 devices: a whole 4x4x16 slice. The times are simulated.
512 devices in a mesh: dp: 64 (over z_lo, y, core), tensor: 8 (over z_hi, x).
Axes of the slice: x: 4, y: 4, z: 16 (z_hi: 2, z_lo: 8; z = z_hi * 8 + z_lo), core: 2. Of those that a mesh axis runs over, the one named last changes fastest.
Arguments:
- query: bfloat16 [8192, 8192], P(('dp', 'tensor')), may hold values from -100 to 100
- key: bfloat16 [8192, 1024], P(('dp', 'tensor')), may hold values from -5 to 5
- value: bfloat16 [8192, 1024], P(('dp', 'tensor')), may hold values from -6 to 6
- output_cotangent: bfloat16 [8192, 8192], P(('dp', 'tensor')), may hold values from -6 to 6
- doc_lengths: int32 [16], replicated, may hold values from 1 to 768, as said below
Outputs:
- attn_out: bfloat16 [8192, 8192], P(('dp', 'tensor'))
- query_grad: bfloat16 [8192, 8192], P(('dp', 'tensor'))
- key_grad: bfloat16 [8192, 1024], P(('dp', 'tensor'))
- value_grad: bfloat16 [8192, 1024], P(('dp', 'tensor'))
Inputs may be any that keep to these rules, and one draw needn't show every extreme that they name: `doc_lengths`: the sum is 8192; the first trajectory is the longest and has exactly 768 tokens.
All inputs are finite; a program needn't handle non-finite values.
Results may differ from a plain program's by a relative error of at most 0.04.
Values may be sent and summed in bfloat16 or wider, within the bound.
A program may use at most 64 MiB of HBM per device.

v0:
```python
import functools
import math

import jax
import jax.numpy as jnp
from jax import lax
from jax.experimental import pallas as pl
from jax.experimental.pallas import tpu as pltpu
from jax.sharding import PartitionSpec as P

D = 128
GROUP = 8
DOCS = 16
SCALE = 1.0 / math.sqrt(D)
LOG2E = math.log2(math.e)
NEG = -1e30
RING = 4
MESH = pl.DeviceIdType.MESH
BF = jnp.bfloat16
F32 = jnp.float32
WIDE = 256
NT = (((1,), (1,)), ((), ()))
NN = (((1,), (0,)), ((), ()))
NEAR = [(dx, dk) for dx in (1, 3, 2, 0) for dk in (0, 1) if (dx, dk) != (0, 0)]


def dot(a, b, dims):
    return lax.dot_general(a, b, dims, preferred_element_type=F32)


def kernel(
    chips, q_in, k_in, v_in, g_in, len_in,
    o_out, dq_out, dk_out, dv_out,
    kvw, mid, qp, gp, qm, gm, sc, pg, pb, db, ret_out, ret_in, tot, far_out, far_in, own_out, own_in, op, qgp,
    way, part_in, part_sum, plane_in, raw, raw_s,
    len_ref, len_s, ring_met, plane_met, near_s, near_r, mid_s, mid_r, q_s, q_r, far_s, far_r, win_s, win_r, ret_s, ret_r, back_s, back_r,
    own_s, own_r, out_s, out_r, way_s, way_r, part_s, part_r, plane_s, plane_r,
):
    d, t = lax.axis_index("dp"), lax.axis_index("tensor")
    c, core, half, x = d // 2, d % 2, t // 4, t % 4
    z_lo, y = c // RING, c % RING
    piece = core * 4 + x
    head = x * 2 + core

    def device(cc, kk, hh, xx):
        return (cc * 2 + kk, hh * 4 + xx)

    def near(dx, dk):
        return (core + dk) % 2, (x + dx) % 4

    def along(by, xx, kk):
        z = (half * 8 + z_lo + by + 16) % 16
        return device(z % 8 * RING + y, kk, z // 8, xx)

    def copy(src, dst, ssem, rsem, to):
        return pltpu.make_async_remote_copy(
            src_ref=src, dst_ref=dst, send_sem=ssem, recv_sem=rsem, device_id=to, device_id_type=MESH
        )

    def landed(ref, sem):
        pltpu.make_async_copy(ref, ref, sem).wait()

    lengths = pltpu.make_async_copy(len_in, len_ref, len_s)
    lengths.start()
    here = [pltpu.make_async_copy((k_in, v_in)[i], raw.at[i], raw_s.at[i]) for i in (0, 1)]
    for cp in here:
        cp.start()
    barrier = pltpu.get_barrier_semaphore()

    def greet(to):
        pl.semaphore_signal(barrier, inc=1, device_id=to, device_id_type=MESH)

    def across(by):
        return device(z_lo * RING + (y + by) % RING, core, half, x)

    for by in (4, -4, 1, -1):
        greet(along(by, x, core))
    for by in (1, 3):
        greet(across(by))
    for dx, dk in NEAR:
        kk, xx = near(dx, dk)
        greet(device(c, kk, half, xx))

    for step in (1, 2, 3):
        @pl.when(c - step < 0)
        def _():
            for hh in (0, 1):
                kvw[hh, step] = jnp.zeros((2, D, D), BF)

        @pl.when(c + step >= chips)
        def _():
            ret_in[1, step - 1] = jnp.zeros((2, D, D), BF)

        @pl.when(y + step >= RING)
        def _():
            ret_in[0, step - 1] = jnp.zeros((2, D, D), BF)

        @pl.when(y - step < 0)
        def _():
            part_in[step - 1] = jnp.zeros((2, D, D), BF)

    takes = (z_lo > 0) & (y > 0)
    gives = (c + RING < chips) & (y > 0)

    @pl.when(jnp.logical_not(gives))
    def _():
        plane_in[...] = jnp.zeros((2, D, D), BF)

    row = lax.broadcasted_iota(jnp.int32, (1, D), 1)
    q_pos = (2 * c + row // 64) * D + half * 64 + row % 64
    start = jnp.zeros((1, D), jnp.int32)
    end = jnp.int32(0)
    lengths.wait()
    for i in range(DOCS):
        end = end + len_ref[i]
        start = jnp.where(q_pos >= end, end, start)
    key_row = lax.broadcasted_iota(jnp.int32, (D, 1), 0)

    def allowed(hh, step):
        which = half if hh == 0 else 1 - half
        k_pos = (2 * (c - step) + key_row // 64) * D + which * 64 + key_row % 64
        ok = k_pos >= start
        if step == 0:
            ok = ok & (k_pos <= q_pos)
        return ok

    pl.semaphore_wait(barrier, 13)

    for by in (1, 3):
        pl.semaphore_signal(ring_met, inc=1, device_id=across(by), device_id_type=MESH)

    sides = [(4, 0), (-4, 1)]
    mine = pl.ds(pl.multiple_of(piece * 16, 16), 16)

    def first_leg(i, by, side):
        cols = pl.ds(side * 4 * D, 4 * D)
        return copy(raw.at[i, :, cols], mid.at[i, :, cols], mid_s.at[i, side], mid_r.at[i, side], along(by, x, core))

    for i in (0, 1):
        here[i].wait()
        for by, side in sides:
            first_leg(i, by, side).start()

    for dx, dk in NEAR:
        kk, xx = near(dx, dk)
        cols = pl.ds(pl.multiple_of((xx * 2 + kk) * D, D), D)
        for i in (0, 1):
            copy(raw.at[i, :, cols], kvw.at[0, 0, i, mine], near_s, near_r,
                 device(c, kk, half, xx)).start()
    cols = pl.ds(pl.multiple_of(head * D, D), D)
    for i in (0, 1):
        pltpu.make_async_copy(raw.at[i, :, cols], kvw.at[0, 0, i, mine], near_r).start()
    pl.semaphore_wait(ring_met, 2)
    pl.semaphore_signal(plane_met, inc=1, device_id=along(-1, x, core), device_id_type=MESH)
    for i, (ref, to) in enumerate(((q_in, qp), (g_in, gp))):
        for dx, dk in NEAR:
            kk, xx = near(dx, dk)
            cols = pl.ds(pl.multiple_of((xx * 2 + kk) * GROUP * D, GROUP * D), GROUP * D)
            copy(ref.at[:, cols], to.at[piece], q_s.at[i], q_r.at[i], device(c, kk, half, xx)).start()
        cols = pl.ds(pl.multiple_of(head * GROUP * D, GROUP * D), GROUP * D)
        pltpu.make_async_copy(ref.at[:, cols], to.at[piece], q_r.at[i]).start()

    landed(kvw.at[0, 0], near_r)
    def window(hh, i, step):
        return copy(kvw.at[hh, 0, i], kvw.at[hh, step, i], win_s.at[hh, i, step - 1], win_r.at[hh, i, step - 1],
                    device(c + step, core, half, x))

    def to_next_plane(i):
        return copy(kvw.at[0, 0, i], way.at[i], way_s.at[i], way_r.at[i], device(c + RING, core, half, x))

    def round_plane(i, back):
        return copy(way.at[i], kvw.at[0, RING - back, i], win_s.at[0, i, 3 - back], win_r.at[0, i, 3 - back],
                    device(c - back, core, half, x))

    def send_window(hh, i):
        if hh == 0:
            pl.when(gives)(to_next_plane(i).start)
        for step in (1, 2, 3):
            pl.when(y + step < RING if hh == 0 else c + step < chips)(window(hh, i, step).start)

    def take_window(hh, i):
        for step in (1, 2, 3):
            pl.when(c - step >= 0)(window(hh, i, step).wait_recv)

    for i in (0, 1):
        send_window(0, i)

    for i in (0, 1):
        for by, side in sides:
            first_leg(i, by, side).wait_recv()
            for j in range(4 * side, 4 * side + 4):
                copy(mid.at[i, :, pl.ds(j * D, D)], kvw.at[1, 0, i, mine], far_s.at[i], far_r.at[i],
                     along(by, j // 2, j % 2)).start()

    for i in (0, 1):
        pl.when(takes)(to_next_plane(i).wait_recv)
        for back in (1, 2, 3):
            pl.when(takes & (y - back >= 0))(round_plane(i, back).start)

    pl.semaphore_wait(plane_met, 1)
    for i in (0, 1):
        landed(kvw.at[1, 0, i], far_r.at[i])
        send_window(1, i)

    def gather(pieces, rows):
        for g in range(GROUP):
            rows[g * D:(g + 1) * D, :] = pieces[:, :, g * D:(g + 1) * D].reshape(D, D)

    landed(qp, q_r.at[0])
    gather(qp, qm)

    lanes = [slice(w * WIDE, (w + 1) * WIDE) for w in range(GROUP * D // WIDE)]
    top = [jnp.full((1, WIDE), NEG, F32) for _ in lanes]
    total = [jnp.zeros((1, WIDE), F32) for _ in lanes]
    groups = [(0, (0,)), (0, (1, 2, 3)), (1, (0,)), (1, (1, 2, 3))]

    def span(hh, steps):
        return slice((hh * 4 + steps[0]) * D, (hh * 4 + steps[-1] + 1) * D)

    def block(hh, steps, i):
        return kvw[hh, steps[0]:steps[-1] + 1, i].reshape(len(steps) * D, D)

    def scores(hh, steps):
        at = span(hh, steps)
        keys = block(hh, steps, 0)
        oks = [jnp.concatenate([allowed(hh, step)] * (WIDE // D), axis=1) for step in steps]
        ok = oks[0] if len(oks) == 1 else jnp.concatenate(oks, axis=0)
        for w, lane in enumerate(lanes):
            s = jnp.where(ok, dot(keys, qm[lane, :], NT) * (SCALE * LOG2E), NEG)
            sc[at, lane] = s
            new = jnp.maximum(top[w], jnp.max(s, axis=0, keepdims=True))
            total[w] = total[w] * jnp.exp2(top[w] - new) + jnp.sum(
                jnp.exp2(sc[at, lane] - new), axis=0, keepdims=True
            )
            top[w] = new

    def prob_grads(hh, steps):
        at = span(hh, steps)
        values = block(hh, steps, 1)
        for lane in lanes:
            pg[at, lane] = dot(values, gm[lane, :], NT)

    landed(gp, q_r.at[1])
    gather(gp, gm)
    for group in (groups[0], groups[2]):
        scores(*group)
        prob_grads(*group)
    for i in (0, 1):
        take_window(0, i)
    scores(*groups[1])
    prob_grads(*groups[1])
    take_window(1, 0)
    scores(*groups[3])

    lse = [top[w] + jnp.log(total[w]) * LOG2E for w in range(len(lanes))]
    mean = [jnp.zeros((1, WIDE), F32) for _ in lanes]

    def probs(hh, steps):
        at = span(hh, steps)
        for w, lane in enumerate(lanes):
            p = jnp.exp2(sc[at, lane] - lse[w])
            sc[at, lane] = p
            pb[at, lane] = p.astype(BF)

    def means(hh, steps):
        at = span(hh, steps)
        for w, lane in enumerate(lanes):
            mean[w] = mean[w] + jnp.sum(sc[at, lane] * pg[at, lane], axis=0, keepdims=True)

    def value_part(hh, steps):
        return dot(pb[span(hh, steps), :], gm[...], NN)

    def score_grads(hh, steps):
        at = span(hh, steps)
        for w, lane in enumerate(lanes):
            db[at, lane] = (sc[at, lane] * (pg[at, lane] - mean[w])).astype(BF)

    def key_part(hh, steps):
        return dot(db[span(hh, steps), :], qm[...], NN)

    def returned(hh, i, step, part=None):
        at, sem = ((hh, step - 1, i), (hh, i, step - 1, 0)) if part is None else (
            (hh, step - 1, i, pl.ds(part * 64, 64)), (hh, i, step - 1, part))
        return copy(ret_out.at[at], ret_in.at[at], ret_s.at[sem], ret_r.at[sem], device(c - step, core, half, x))

    halves = (0, 1)

    def in_plane(i, ahead):
        return copy(ret_out.at[0, 3 - ahead, i], part_in.at[ahead - 1, i], part_s.at[i, ahead - 1],
                    part_r.at[i, ahead - 1], device(c + ahead, core, half, x))

    def to_last_plane(i):
        return copy(part_sum.at[i], plane_in.at[i], plane_s.at[i], plane_r.at[i], device(c - RING, core, half, x))

    def send_back(hh, i, part):
        ret_out[hh, :, i] = part.astype(BF).reshape(3, D, D)
        for step in (1, 2, 3):
            if hh == 0:
                ahead = RING - step
                pl.when((z_lo > 0) & (y + ahead < RING))(in_plane(i, ahead).start)
                pl.when(y - step >= 0)(returned(hh, i, step).start)
            else:
                for chunk in halves:
                    pl.when(c - step >= 0)(returned(hh, i, step, chunk).start)

    def pass_back(i):
        for ahead in (1, 2, 3):
            pl.when(takes & (y - ahead >= 0))(in_plane(i, ahead).wait_recv)

        @pl.when(takes)
        def _():
            part = part_in[0, i].astype(F32)
            for ahead in (2, 3):
                part = part + part_in[ahead - 1, i].astype(F32)
            part_sum[i] = part.astype(BF)
            to_last_plane(i).start()

    def spread(which, i, weights, pieces, out, factor):
        blocks = kvw[:, :, i].reshape(8 * D, D).T
        full = dot(blocks, weights[...], NN)
        if factor != 1.0:
            full = full * factor
        for g in range(GROUP):
            pieces[:, :, g * D:(g + 1) * D] = full[:, g * D:(g + 1) * D].T.astype(BF).reshape(8, 16, D)
        cols = pl.ds(pl.multiple_of(head * GROUP * D, GROUP * D), GROUP * D)
        for dx, dk in NEAR:
            kk, xx = near(dx, dk)
            copy(pieces.at[kk * 4 + xx], out.at[:, cols], out_s.at[which], out_r.at[which],
                 device(c, kk, half, xx)).start()
        pltpu.make_async_copy(pieces.at[piece], out.at[:, cols], out_r.at[which]).start()

    def total_of(i):
        for step in (1, 2, 3):
            pl.when(y + step < RING)(returned(0, i, step).wait_recv)
        pl.when(gives)(to_last_plane(i).wait_recv)
        part = tot[0, i] + plane_in[i].astype(F32)
        for step in (1, 2, 3):
            part = part + ret_in[0, step - 1, i].astype(F32)
        return part.astype(BF)

    def cross(i, which):
        for step in (1, 2, 3):
            pl.when(c + step < chips)(returned(1, i, step, which).wait_recv)
        rows = slice(which * 64, which * 64 + 64)
        part = tot[1, i, rows]
        for step in (1, 2, 3):
            part = part + ret_in[1, step - 1, i, rows].astype(F32)
        far_out[i, rows] = part.astype(BF)
        for p in range(which * 4, which * 4 + 4):
            copy(far_out.at[i, pl.ds(p * 16, 16)], far_in.at[i, pl.ds(pl.multiple_of(head * 16, 16), 16)],
                 back_s.at[i], back_r.at[i], along(8, p % 4, p // 4)).start()

    probs(*groups[3])
    send_back(1, 1, value_part(*groups[3]))
    for group in groups[:3]:
        probs(*group)
        means(*group)
    take_window(1, 1)
    prob_grads(*groups[3])
    means(*groups[3])
    for chunk in halves:
        first = [(5 + n) * D + chunk * 64 for n in range(3)]
        for at in first:
            at = slice(at, at + 64)
            for w, lane in enumerate(lanes):
                db[at, lane] = (sc[at, lane] * (pg[at, lane] - mean[w])).astype(BF)
        grads = dot(jnp.concatenate([db[at:at + 64, :] for at in first], axis=0), qm[...], NN).astype(BF)
        for step in (1, 2, 3):
            ret_out[1, step - 1, 0, chunk * 64:chunk * 64 + 64] = grads[(step - 1) * 64:step * 64]
            pl.when(c - step >= 0)(returned(1, 0, step, chunk).start)
    send_back(0, 1, value_part(*groups[1]))
    score_grads(*groups[1])
    send_back(0, 0, key_part(*groups[1]))
    tot[1, 1] = value_part(*groups[2])
    score_grads(*groups[2])
    tot[1, 0] = key_part(*groups[2])
    cross(1, 0)
    cross(1, 1)
    pl.when(half == 0)(lambda: pass_back(1))
    spread(0, 1, pb, op, o_out, 1.0)
    pl.when(half == 0)(lambda: pass_back(0))

    @pl.when(half == 1)
    def _():
        cross(0, 0)
        cross(0, 1)
        pass_back(1)
        pass_back(0)

    score_grads(*groups[0])
    spread(1, 0, db, qgp, dq_out, SCALE)
    tot[0, 1] = value_part(*groups[0])
    tot[0, 0] = key_part(*groups[0])
    to = pl.ds(pl.multiple_of(head * 16, 16), 16)
    for i in (1, 0):
        own_out[i] = total_of(i)
        for dx, dk in NEAR:
            kk, xx = near(dx, dk)
            copy(own_out.at[i, pl.ds(pl.multiple_of((kk * 4 + xx) * 16, 16), 16)], own_in.at[i, to], own_s.at[i],
                 own_r.at[i], device(c, kk, half, xx)).start()
        pltpu.make_async_copy(own_out.at[i, mine], own_in.at[i, to], own_r.at[i]).start()
    @pl.when(half == 0)
    def _():
        cross(0, 0)
        cross(0, 1)

    for i, (out, factor) in ((1, (dv_out, 1.0)), (0, (dk_out, SCALE))):
        landed(own_in.at[i], own_r.at[i])
        landed(far_in.at[i], back_r.at[i])
        for j in range(8):
            both = own_in[i, j * 16:(j + 1) * 16].astype(F32) + far_in[i, j * 16:(j + 1) * 16].astype(F32)
            out[:, j * D:(j + 1) * D] = (both * factor).astype(BF)

    landed(kvw.at[0, 0, :, pl.ds(0, 112)], near_s)
    for i, ref in enumerate((qp, gp)):
        landed(ref.at[pl.ds(0, 7)], q_s.at[i])
    for i in (0, 1):
        for by, side in sides:
            first_leg(i, by, side).wait_send()
        landed(kvw.at[1, 0, i], far_s.at[i])
        pl.when(gives)(to_next_plane(i).wait_send)
        pl.when(takes)(to_last_plane(i).wait_send)
        for step in (1, 2, 3):
            pl.when(y + step < RING)(window(0, i, step).wait_send)
            pl.when(takes & (y - step >= 0))(round_plane(i, step).wait_send)
            pl.when(c + step < chips)(window(1, i, step).wait_send)
            pl.when((z_lo > 0) & (y + step < RING))(in_plane(i, step).wait_send)
            pl.when(y - step >= 0)(returned(0, i, step).wait_send)
            for chunk in halves:
                pl.when(c - step >= 0)(returned(1, i, step, chunk).wait_send)
        landed(far_out.at[i], back_s.at[i])
        landed(own_out.at[i, pl.ds(0, 112)], own_s.at[i])
    for i, ref in enumerate((op, qgp)):
        landed(ref.at[pl.ds(0, 7)], out_s.at[i])
    for i, ref in enumerate((o_out, dq_out)):
        landed(ref, out_r.at[i])


def write_out(a, b, c, d, ao, bo, co, do, sems):
    copies = [
        pltpu.make_async_copy(src, dst, sems.at[i]) for i, (src, dst) in enumerate(((a, ao), (b, bo), (c, co), (d, do)))
    ]
    for cp in copies:
        cp.start()
    for cp in copies:
        cp.wait()


def per_device(query, key, value, cotangent, doc_lengths):
    chips = lax.axis_size("dp") // 2
    rows = GROUP * D
    keys = 8 * D
    sem = pltpu.SemaphoreType.DMA
    any_ = pl.BlockSpec(memory_space=pl.ANY)
    vmem = pl.BlockSpec(memory_space=pltpu.VMEM)
    parts = pl.pallas_call(
        functools.partial(kernel, chips),
        out_shape=[jax.ShapeDtypeStruct(a.shape, BF) for a in (query, query, key, value)],
        in_specs=[any_] * 5,
        out_specs=[vmem] * 4,
        scratch_shapes=[
            pltpu.VMEM((2, 4, 2, D, D), BF),
            pltpu.VMEM((2, 16, 8 * D), BF),
            pltpu.VMEM((8, 16, rows), BF),
            pltpu.VMEM((8, 16, rows), BF),
            pltpu.VMEM((rows, D), BF),
            pltpu.VMEM((rows, D), BF),
            pltpu.VMEM((keys, rows), F32),
            pltpu.VMEM((keys, rows), F32),
            pltpu.VMEM((keys, rows), BF),
            pltpu.VMEM((keys, rows), BF),
            pltpu.VMEM((2, 3, 2, D, D), BF),
            pltpu.VMEM((2, 3, 2, D, D), BF),
            pltpu.VMEM((2, 2, D, D), F32),
            pltpu.VMEM((2, D, D), BF),
            pltpu.VMEM((2, D, D), BF),
            pltpu.VMEM((2, D, D), BF),
            pltpu.VMEM((2, D, D), BF),
            pltpu.VMEM((8, 16, rows), BF),
            pltpu.VMEM((8, 16, rows), BF),
            pltpu.VMEM((2, D, D), BF),
            pltpu.VMEM((3, 2, D, D), BF),
            pltpu.VMEM((2, D, D), BF),
            pltpu.VMEM((2, D, D), BF),
            pltpu.VMEM((2, 16, 8 * D), BF), sem((2,)),
            pltpu.SMEM((DOCS,), jnp.int32), sem, pltpu.SemaphoreType.REGULAR, pltpu.SemaphoreType.REGULAR,
            sem, sem, sem((2, 2)), sem((2, 2)), sem((2,)), sem((2,)), sem((2,)), sem((2,)),
            sem((2, 2, 3)), sem((2, 2, 3)), sem((2, 2, 3, 2)), sem((2, 2, 3, 2)),
            sem((2,)), sem((2,)), sem((2,)), sem((2,)), sem((2,)), sem((2,)),
            sem((2,)), sem((2,)), sem((2, 3)), sem((2, 3)), sem((2,)), sem((2,)),
        ],
        compiler_params=pltpu.CompilerParams(
            collective_id=0, has_side_effects=True, vmem_limit_bytes=60 << 20
        ),
        name="attention",
    )(query, key, value, cotangent, doc_lengths)
    return pl.pallas_call(
        write_out,
        out_shape=[jax.ShapeDtypeStruct(a.shape, BF) for a in parts],
        in_specs=[vmem] * 4,
        out_specs=[any_] * 4,
        scratch_shapes=[sem((4,))],
        name="write_out",
    )(*parts)


def solution(mesh):
    placed = P(("dp", "tensor"), None)
    return jax.shard_map(
        per_device,
        mesh=mesh,
        in_specs=(placed,) * 4 + (P(),),
        out_specs=(placed,) * 4,
        check_vma=False,
    )
```

profile of v0, /device:TPU:41, one launch (start us, length us, event | category | flops | bytes accessed | tf_op | source)
XLA Modules:
  0.0 51.8 jit_solution(541877814827585420)
XLA Ops:
  0.6 49.3 %attention.1 = (bf16[16,8192]{1,0:T(8,128)(2,1)}, bf16[16,8192]{1,0:T(8,128)(2,1)}, bf16[16,1024]{1,0:T(8,128)(2,1)}, bf16[16,1024]{1,0:T(8,128)(2,1)}) custom-call(bf16[16,8192]{1,0:T(8,128)(2,1)} %q_in.1, bf16[16,1024]{1,0:T(8,128)(2,1)} %k_in.1, bf16[16,1024]{1,0:T(8,128)(2,1)} %v_in.1, bf16[16,8192]{1,0:T(8,128)(2,1)} %g_in.1, s32[16]{0:T(128)} %len_in.1), custom_call_target="tpu_custom_call" | custom-call | tf_op jit(solution)/shard_map/attention/pallas_call | solution.py:456
  49.9 1.9 %write_out.1 = (bf16[16,8192]{1,0:T(8,128)(2,1)}, bf16[16,8192]{1,0:T(8,128)(2,1)}, bf16[16,1024]{1,0:T(8,128)(2,1)}, bf16[16,1024]{1,0:T(8,128)(2,1)}) custom-call(bf16[16,8192]{1,0:T(8,128)(2,1)} %get-tuple-element.8.a, bf16[16,8192]{1,0:T(8,128)(2,1)} %get-tuple-element.9.b, bf16[16,1024]{1,0:T(8,128)(2,1)} %get-tuple-element.10.c, ...), custom_call_target="tpu_custom_call" | custom-call | tf_op jit(solution)/shard_map/write_out/pallas_call | solution.py:497
where the time goes:
time: 52 us; the launch traced here: 51.8 us
  Pallas kernels  51.2 us (98%)
  between operations  0.64 us (1%)
    pallas_call x1, Pallas kernels, per_device(): pl.pallas_call(functools.partial(kernel, chips), out_shape=[jax.ShapeDtyp...  49.3 us
    pallas_call x1, Pallas kernels, per_device(): pl.pallas_call(write_out, out_shape=[jax.ShapeDtypeStruct(a.shape, BF) fo...  1.87 us

commit v1 on v0

--- a/solution.py
+++ b/solution.py
@@ -160,6 +160,14 @@
         cols = pl.ds(pl.multiple_of(head * GROUP * D, GROUP * D), GROUP * D)
         pltpu.make_async_copy(ref.at[:, cols], to.at[piece], q_r.at[i]).start()
 
+    for i in (0, 1):
+        for by, side in sides:
+            first_leg(i, by, side).wait_recv()
+        for by, side in sides:
+            for j in range(4 * side, 4 * side + 4):
+                copy(mid.at[i, :, pl.ds(j * D, D)], kvw.at[1, 0, i, mine], far_s.at[i], far_r.at[i],
+                     along(by, j // 2, j % 2)).start()
+
     landed(kvw.at[0, 0], near_r)
     def window(hh, i, step):
         return copy(kvw.at[hh, 0, i], kvw.at[hh, step, i], win_s.at[hh, i, step - 1], win_r.at[hh, i, step - 1],
@@ -184,13 +192,6 @@
 
     for i in (0, 1):
         send_window(0, i)
-
-    for i in (0, 1):
-        for by, side in sides:
-            first_leg(i, by, side).wait_recv()
-            for j in range(4 * side, 4 * side + 4):
-                copy(mid.at[i, :, pl.ds(j * D, D)], kvw.at[1, 0, i, mine], far_s.at[i], far_r.at[i],
-                     along(by, j // 2, j % 2)).start()
 
     for i in (0, 1):
         pl.when(takes)(to_next_plane(i).wait_recv)

time: 52 us -> 52.1 us (level)
  the two profiles are of different devices: /device:TPU:41 before, /device:TPU:9 now
where the time goes in v1:
time: 52.1 us; the launch traced here: 51.9 us
  Pallas kernels  51.3 us (98%)
  between operations  0.64 us (1%)
    pallas_call x1, Pallas kernels, per_device(): pl.pallas_call(functools.partial(kernel, chips), out_shape=[jax.ShapeDtyp...  49.4 us
    pallas_call x1, Pallas kernels, per_device(): pl.pallas_call(write_out, out_shape=[jax.ShapeDtypeStruct(a.shape, BF) fo...  1.87 us

profile of v1, /device:TPU:9, one launch (start us, length us, event | category | flops | bytes accessed | tf_op | source)
XLA Modules:
  0.0 51.9 jit_solution(1813820998579454746)
XLA Ops:
  0.6 49.4 %attention.1 = (bf16[16,8192]{1,0:T(8,128)(2,1)}, bf16[16,8192]{1,0:T(8,128)(2,1)}, bf16[16,1024]{1,0:T(8,128)(2,1)}, bf16[16,1024]{1,0:T(8,128)(2,1)}) custom-call(bf16[16,8192]{1,0:T(8,128)(2,1)} %q_in.1, bf16[16,1024]{1,0:T(8,128)(2,1)} %k_in.1, bf16[16,1024]{1,0:T(8,128)(2,1)} %v_in.1, bf16[16,8192]{1,0:T(8,128)(2,1)} %g_in.1, s32[16]{0:T(128)} %len_in.1), custom_call_target="tpu_custom_call" | custom-call | tf_op jit(solution)/shard_map/attention/pallas_call | solution.py:457
  50.1 1.9 %write_out.1 = (bf16[16,8192]{1,0:T(8,128)(2,1)}, bf16[16,8192]{1,0:T(8,128)(2,1)}, bf16[16,1024]{1,0:T(8,128)(2,1)}, bf16[16,1024]{1,0:T(8,128)(2,1)}) custom-call(bf16[16,8192]{1,0:T(8,128)(2,1)} %get-tuple-element.8.a, bf16[16,8192]{1,0:T(8,128)(2,1)} %get-tuple-element.9.b, bf16[16,1024]{1,0:T(8,128)(2,1)} %get-tuple-element.10.c, ...), custom_call_target="tpu_custom_call" | custom-call | tf_op jit(solution)/shard_map/write_out/pallas_call | solution.py:498
